TPU v7x, 32 devices: a whole 2x2x4 slice. The times are simulated.
32 devices in a mesh: rec: 16 (over z, y, x), var: 2 (over core).
Axes of the slice: x: 2, y: 2, z: 4, core: 2. Of those that a mesh axis runs over, the one named last changes fastest.
Arguments:
- records: bfloat16 [32768, 8192], P('rec', 'var'), as said below
- test_matrix: bfloat16 [8192, 256], P('var'), may hold values from -0.0625 to 0.0625
- col_types: int32 [8192], P('var'), may hold values from 0 to 1
- col_groups: int32 [8192], P('var'), may hold values from 0 to 15
- group_weight: float32 [16], replicated, may hold values from 0.5 to 2
Outputs:
- scores_basis: bfloat16 [32768, 256], P(('rec', 'var'))
- projection: bfloat16 [256, 8192], P(None, 'var')
Inputs may be any that keep to these rules, and one draw needn't show every extreme that they name: `records`: every entry is positive.
All inputs are finite; a program needn't handle non-finite values.
Results may differ from a plain program's by a relative error of at most 0.0043.
The roundings to bfloat16 on the way count: a program that leaves them out, or rounds other values in their place, can miss the bound.
Values sent between devices are 32-bit elements; how exact they have to be, the bound alone decides.
A program may use at most 64 MiB of HBM per device.

v0:
```python
import math
import jax
import jax.numpy as jnp
from jax import lax
from jax.sharding import PartitionSpec as P

epsilon = 1e-05
highest = lax.Precision.HIGHEST


def column_factor(col_mean, col_square, col_types, col_weight):
    spread = col_square - col_mean * col_mean
    picked = jnp.where(col_types == 1, lax.rsqrt(col_mean + epsilon), lax.rsqrt(spread + epsilon))
    return picked * col_weight


def row_gram(left, right):
    return lax.dot_general(
        left, right, (((1,), (1,)), ((), ())), precision=highest, preferred_element_type=jnp.float32
    )


def lower_solve(lower, right):
    return lax.linalg.triangular_solve(lower, right, left_side=True, lower=True)


def local(records, test_matrix, col_types, col_groups, group_weight):
    total_rows = records.shape[0] * lax.axis_size("rec")
    values = records.astype(jnp.float32)
    col_sum, col_square = lax.psum((jnp.sum(values, 0), jnp.sum(values * values, 0)), "rec")
    col_mean = col_sum / total_rows
    onehot = (
        col_groups[:, None] == jnp.arange(group_weight.shape[0], dtype=jnp.int32)[None, :]
    ).astype(jnp.float32)
    col_weight = jnp.dot(onehot, group_weight, precision=highest)
    factor = column_factor(col_mean, col_square / total_rows, col_types, col_weight)
    scaled = ((values - col_mean) * factor).astype(jnp.bfloat16)
    partial_sketch = lax.dot_general(
        test_matrix, scaled, (((0,), (1,)), ((), ())), preferred_element_type=jnp.float32
    )
    piece_len = records.shape[0] // lax.axis_size("var")
    sketch = lax.psum(partial_sketch, "var")
    own_rows = lax.dynamic_slice_in_dim(sketch, lax.axis_index("var") * piece_len, piece_len, 1)
    factor_lower = jnp.linalg.cholesky(lax.psum(row_gram(own_rows, own_rows), ("rec", "var")))
    basis_own = lower_solve(factor_lower, own_rows)
    whole_basis = lower_solve(factor_lower, sketch)
    result = jnp.dot(whole_basis, scaled, precision=highest, preferred_element_type=jnp.float32)
    summed = lax.psum(result, "rec")
    summed = summed / math.sqrt(total_rows)
    scores_basis = (basis_own.T * math.sqrt(total_rows)).astype(jnp.bfloat16)
    return (scores_basis, summed.astype(jnp.bfloat16))


def solution(mesh):
    in_specs = (P("rec", "var"), P("var", None), P("var"), P("var"), P())
    out_specs = (P(("rec", "var"), None), P(None, "var"))
    return jax.shard_map(local, mesh=mesh, in_specs=in_specs, out_specs=out_specs, check_vma=False)
```

profile of v0, /device:TPU:0, one launch (start us, length us, event | category | flops | bytes accessed | tf_op | source)
XLA Modules:
  0.0 518.7 jit_solution(11401620359540813519)
XLA Ops:
  7.2 0.0 copy-start
  7.2 0.0 copy-start.3
  7.2 0.0 copy-start.2
  7.2 0.0 copy-start.1
  7.2 0.0 all-reduce.6.cloned.1.call-start
  7.3 7.7 %convert_reduce_fusion = (f32[4096]{0:T(1024)S(1)}, f32[4096]{0:T(1024)S(1)}) fusion(bf16[2048,4096]{1,0:T(8,128)(2,1)} %param.5), kind=kLoop, calls=%fused_computation.4 | loop fusion | flops 33546240 | bytes 16809984 | tf_op jit(solution)/shard_map/reduce_sum | solution.py:30
  15.0 0.0 copy-done.3
  15.0 0.0 copy-done.2
  15.0 0.2 fusion.22
  15.2 78.6 %all-reduce.1 = (f32[4096]{0:T(1024)S(1)}, f32[4096]{0:T(1024)S(1)}) all-reduce(f32[4096]{0:T(1024)S(1)} %get-tuple-element.15, f32[4096]{0:T(1024)S(1)} %get-tuple-element.14), channel_id=1, replica_groups=mesh['rec'=16,'var'=2] {'rec'}, use_global_device_ids=true, to_apply=%region_3.0 | all-reduce | flops 8192 | bytes 65536 | tf_op jit(solution)/shard_map/psum | solution.py:30
  93.8 0.0 copy-done.1
  93.8 0.0 copy-done
  93.8 9.9 %fusion.7 = f32[256,2048]{0,1:T(8,128)} fusion(bf16[4096,256]{1,0:T(8,128)(2,1)S(1)} %copy-done, bf16[2048,4096]{1,0:T(8,128)(2,1)} %param.5, f32[4096]{0:T(1024)S(1)} %get-tuple-element.33, f32[4096]{0:T(1024)S(1)} %get-tuple-element.32), kind=kOutput, calls=%fused_computation.11 | convolution fusion | flops 4328521728 | bytes 21004288 | tf_op jit(solution)/shard_map/dot_general | solution.py:38
  103.7 0.0 all-reduce.6.cloned.1.call-update
  103.7 0.0 all-reduce.8.cloned.1.call-start
  103.8 17.2 %all-reduce.6.cloned.1.call-done = f32[256,2048]{0,1:T(8,128)} async-done(((f32[256,2048]{0,1:T(8,128)}), f32[256,2048]{0,1:T(8,128)}) %all-reduce.6.cloned.1.call-update) | async-done | bytes 2097168 | tf_op jit(solution)/shard_map/psum | solution.py:42
  120.9 4.2 fusion.16
  125.2 0.0 all-reduce.8.cloned.1.call-update
  125.2 0.2 all-reduce.10.cloned.1.call-start
  125.5 128.7 %all-reduce.8.cloned.1.call-done = f32[256,256]{0,1:T(8,128)} async-done(((f32[256,256]{0,1:T(8,128)}), f32[256,256]{0,1:T(8,128)}) %all-reduce.8.cloned.1.call-update) | async-done | bytes 262160 | tf_op jit(solution)/shard_map/psum | solution.py:44
  254.2 1.1 copy.11
  255.3 1.0 fusion.21
  256.3 11.7 %cholesky.50 = f32[128,128]{1,0:T(8,128)S(1)} custom-call(f32[128,128]{1,0:T(8,128)S(1)} %cholesky.118), custom_call_target="Cholesky" | custom-call | tf_op jit(solution)/shard_map/jit(cholesky)/cholesky | solution.py:44
  268.0 9.8 %custom-call.16 = f32[1,128,128]{1,2,0:T(8,128)S(1)} custom-call(f32[1,128,128]{2,1,0:T(8,128)S(1)} %get-tuple-element.31), custom_call_target="InvertDiagBlocksLowerTriangular" | custom-call | tf_op jit(solution)/shard_map/jit(cholesky)/cholesky | solution.py:44
  277.9 0.2 constant_dynamic-update-slice_fusion
  278.1 0.3 convolution_subtract_fusion.2
  278.4 11.7 %cholesky.105 = f32[128,128]{1,0:T(8,128)S(1)} custom-call(f32[128,128]{1,0:T(8,128)S(1)} %convolution_subtract_fusion.2), custom_call_target="Cholesky" | custom-call | tf_op jit(solution)/shard_map/jit(cholesky)/cholesky | solution.py:44
  290.1 0.7 compare_reduce_fusion
  292.2 0.1 triangular_solve.72
  292.3 4.3 while.1
  292.5 0.6 fusion.44
  293.1 1.4 bitcast_dynamic-update-slice_fusion.2
  294.5 0.6 fusion.44
  295.1 1.4 bitcast_dynamic-update-slice_fusion.2
  296.6 19.7 %custom-call.17 = f32[2,128,128]{1,2,0:T(8,128)S(1)} custom-call(f32[2,128,128]{2,1,0:T(8,128)S(1)} %get-tuple-element.9), custom_call_target="InvertDiagBlocksLowerTriangular" | custom-call | tf_op jit(solution)/shard_map/triangular_solve | solution.py:24
  316.3 2.3 fusion.13
  318.6 3.0 convolution_subtract_fusion
  321.6 1.1 fusion.27
  322.7 18.2 %fusion.3 = f32[256,4096]{1,0:T(8,128)} fusion(bf16[2048,4096]{1,0:T(8,128)(2,1)} %param.5, f32[4096]{0:T(1024)S(1)} %get-tuple-element.33, f32[4096]{0:T(1024)S(1)} %get-tuple-element.32, f32[128,2048]{1,0:T(8,128)S(1)} %fusion.27, f32[128,2048]{1,0:T(8,128)S(1)} %fusion.13), kind=kOutput, calls=%fused_computation.8 | convolution fusion | flops 25803882496 | bytes 23101440 | tf_op jit(solution)/shard_map/dot_general | solution.py:47
  340.9 0.0 all-reduce.10.cloned.1.call-update
  340.9 1.7 fusion.19
  342.6 2.0 convolution_subtract_fusion.1
  344.7 0.6 fusion.28
  345.3 0.1 fusion.18
  345.4 1.0 copy.12
  346.4 161.8 %all-reduce.10.cloned.1.call-done = f32[256,4096]{1,0:T(8,128)} async-done(((f32[256,4096]{1,0:T(8,128)}), f32[256,4096]{1,0:T(8,128)}) %all-reduce.10.cloned.1.call-update) | async-done | bytes 4194320 | tf_op jit(solution)/shard_map/psum | solution.py:48
  508.3 3.9 multiply_convert_fusion
  (10 shorter events, 0.2 us)
Async XLA Ops:
  7.2 86.6 %copy-start = (bf16[4096,256]{1,0:T(8,128)(2,1)S(1)}, bf16[4096,256]{1,0:T(8,128)(2,1)}, u32[]{:S(2)}) copy-start(bf16[4096,256]{1,0:T(8,128)(2,1)} %param.6) | copy-start | bytes 6291460
  7.2 7.8 %copy-start.3 = (f32[16]{0:T(128)S(1)}, f32[16]{0:T(128)}, u32[]{:S(2)}) copy-start(f32[16]{0:T(128)} %param.9) | copy-start | bytes 196
  7.2 7.8 %copy-start.2 = (s32[4096]{0:T(1024)S(1)}, s32[4096]{0:T(1024)}, u32[]{:S(2)}) copy-start(s32[4096]{0:T(1024)} %param.8) | copy-start | bytes 49156
  7.2 86.6 %copy-start.1 = (s32[4096]{0:T(1024)S(1)}, s32[4096]{0:T(1024)}, u32[]{:S(2)}) copy-start(s32[4096]{0:T(1024)} %param.7) | copy-start | bytes 49156
  7.2 113.7 %all-reduce.6.cloned.1.call-start = ((), (), s32[]{:S(2)}) async-start(), calls=%async_computation | async-start | bytes 4194304 | tf_op jit(solution)/shard_map/psum | solution.py:42
  103.7 150.5 %all-reduce.8.cloned.1.call-start = ((), (), s32[]{:S(2)}) async-start(), calls=%async_computation.1 | async-start | bytes 524288 | tf_op jit(solution)/shard_map/psum | solution.py:44
  125.2 383.1 %all-reduce.10.cloned.1.call-start = ((), (), s32[]{:S(2)}) async-start(), calls=%async_computation.2 | async-start | bytes 8388608 | tf_op jit(solution)/shard_map/psum | solution.py:48
Sparse Core Ops, SparseCore 0:
  103.8 17.0 all-reduce.5
  127.9 126.2 all-reduce.7
  341.1 167.1 all-reduce.9
where the time goes:
time: 519 us
  waiting for transfers between devices  308 us (59%)
  blocking collectives  78.6 us (15%)
  other arithmetic  66.4 us (13%)
  matrix products  43.8 us (8%)
  between operations  15.3 us (3%)
  local copies, waits for them, and re-layouts  6.25 us (1%)
    psum x1, waiting for transfers between devices, local(): summed = lax.psum(result, 'rec')  162 us
    psum x1, waiting for transfers between devices, local(): lax.psum(row_gram(own_rows, own_rows), ('rec', 'var'))  129 us
    psum x1, blocking collectives, local(): lax.psum((jnp.sum(values, 0), jnp.sum(values * values, 0)), 'rec')  78.6 us
    another operation x6, other arithmetic, local(): jnp.linalg.cholesky(lax.psum(row_gram(own_rows, own_rows), ('rec', 'var')))  34 us
    another operation x3, other arithmetic, lower_solve(): return lax.linalg.triangular_solve(lower, right, left_side=True, lower=True)  19.7 us
    dot_general x1, matrix products, local(): jnp.dot(whole_basis, scaled, precision=highest, preferred_element_type=jn...  18.2 us
    psum x1, waiting for transfers between devices, local(): sketch = lax.psum(partial_sketch, 'var')  17.2 us
    another operation x6, matrix products, lower_solve(): return lax.linalg.triangular_solve(lower, right, left_side=True, lower=True)  10.8 us
  transfers between devices with their start and end apart: 3, of which 3 were waited for; matrix products, arithmetic and copies ran while one was open for 1% of the time, Pallas kernels for 0%

commit v1 on v0

--- a/solution.py
+++ b/solution.py
@@ -41,7 +41,9 @@
     piece_len = records.shape[0] // lax.axis_size("var")
     sketch = lax.psum(partial_sketch, "var")
     own_rows = lax.dynamic_slice_in_dim(sketch, lax.axis_index("var") * piece_len, piece_len, 1)
-    factor_lower = jnp.linalg.cholesky(lax.psum(row_gram(own_rows, own_rows), ("rec", "var")))
+    factor_lower = jnp.linalg.cholesky(
+        jnp.sum(lax.all_gather(row_gram(own_rows, own_rows), ("rec", "var")), axis=0)
+    )
     basis_own = lower_solve(factor_lower, own_rows)
     whole_basis = lower_solve(factor_lower, sketch)
     result = jnp.dot(whole_basis, scaled, precision=highest, preferred_element_type=jnp.float32)

time: 519 us -> 471 us (0.908)
  waiting for transfers between devices: 308 us -> 257 us
    psum x1 -> x0, waiting for transfers between devices: 129 us -> none  [local(): lax.psum(row_gram(own_rows, own_rows), ('rec', 'var'))]
    all_gather x0 -> x1, waiting for transfers between devices: none -> 78.5 us  [local(): lax.all_gather(row_gram(own_rows, own_rows), ('rec', 'var'))]
where the time goes in v1:
time: 471 us; the launch traced here: 470 us
  waiting for transfers between devices  257 us (55%)
  blocking collectives  78.6 us (17%)
  other arithmetic  69.4 us (15%)
  matrix products  43.8 us (9%)
  between operations  15.3 us (3%)
  local copies, waits for them, and re-layouts  5.3 us (1%)
    psum x1, waiting for transfers between devices, local(): summed = lax.psum(result, 'rec')  161 us
    psum x1, blocking collectives, local(): lax.psum((jnp.sum(values, 0), jnp.sum(values * values, 0)), 'rec')  78.6 us
    all_gather x1, waiting for transfers between devices, local(): lax.all_gather(row_gram(own_rows, own_rows), ('rec', 'var'))  78.5 us
    another operation x6, other arithmetic, local(): jnp.linalg.cholesky(jnp.sum(lax.all_gather(row_gram(own_rows, own_rows),...  34 us
    another operation x3, other arithmetic, lower_solve(): return lax.linalg.triangular_solve(lower, right, left_side=True, lower=True)  19.7 us
    dot_general x1, matrix products, local(): jnp.dot(whole_basis, scaled, precision=highest, preferred_element_type=jn...  18.2 us
    psum x1, waiting for transfers between devices, local(): sketch = lax.psum(partial_sketch, 'var')  17.2 us
    another operation x6, matrix products, lower_solve(): return lax.linalg.triangular_solve(lower, right, left_side=True, lower=True)  10.8 us
  transfers between devices with their start and end apart: 3, of which 3 were waited for; matrix products, arithmetic and copies ran while one was open for 1% of the time, Pallas kernels for 0%

profile of v1, /device:TPU:0, one launch (start us, length us, event | category | flops | bytes accessed | tf_op | source)
XLA Modules:
  0.0 470.1 jit_solution(17558287568567297276)
XLA Ops:
  7.2 0.0 copy-start
  7.2 0.0 copy-start.2
  7.2 0.0 copy-start.3
  7.2 0.0 copy-start.1
  7.2 0.0 all-reduce.5.cloned.1.call-start
  7.3 7.7 %convert_reduce_fusion = (f32[4096]{0:T(1024)S(1)}, f32[4096]{0:T(1024)S(1)}) fusion(bf16[2048,4096]{1,0:T(8,128)(2,1)} %param.5), kind=kLoop, calls=%fused_computation.4 | loop fusion | flops 33546240 | bytes 16809984 | tf_op jit(solution)/shard_map/reduce_sum | solution.py:30
  15.0 78.6 %all-reduce.1 = (f32[4096]{0:T(1024)S(1)}, f32[4096]{0:T(1024)S(1)}) all-reduce(f32[4096]{0:T(1024)S(1)} %get-tuple-element.17, f32[4096]{0:T(1024)S(1)} %get-tuple-element.16), channel_id=1, replica_groups=mesh['rec'=16,'var'=2] {'rec'}, use_global_device_ids=true, to_apply=%region_3.0 | all-reduce | flops 8192 | bytes 65536 | tf_op jit(solution)/shard_map/psum | solution.py:30
  93.5 0.0 copy-done.2
  93.5 0.0 copy-done.3
  93.6 0.2 fusion.22
  93.8 0.0 copy-done.1
  93.8 0.0 copy-done
  93.8 9.9 %fusion.7 = f32[256,2048]{0,1:T(8,128)} fusion(bf16[4096,256]{1,0:T(8,128)(2,1)S(1)} %copy-done, bf16[2048,4096]{1,0:T(8,128)(2,1)} %param.5, f32[4096]{0:T(1024)S(1)} %get-tuple-element.35, f32[4096]{0:T(1024)S(1)} %get-tuple-element.34), kind=kOutput, calls=%fused_computation.11 | convolution fusion | flops 4328521728 | bytes 21004288 | tf_op jit(solution)/shard_map/dot_general | solution.py:38
  103.7 0.0 all-reduce.5.cloned.1.call-update
  103.7 0.0 all-gather.3.cloned.1.call-start
  103.8 17.2 %all-reduce.5.cloned.1.call-done = f32[256,2048]{0,1:T(8,128)} async-done(((f32[256,2048]{0,1:T(8,128)}), f32[256,2048]{0,1:T(8,128)}) %all-reduce.5.cloned.1.call-update) | async-done | bytes 2097168 | tf_op jit(solution)/shard_map/psum | solution.py:42
  121.0 4.3 fusion.16
  125.2 0.0 all-gather.3.cloned.1.call-update
  125.2 0.2 all-reduce.7.cloned.1.call-start
  125.5 78.5 %all-gather.3.cloned.1.call-done = f32[8192,256]{1,0:T(8,128)} async-done(((f32[256,256]{1,0:T(8,128)}), f32[8192,256]{1,0:T(8,128)}) %all-gather.3.cloned.1.call-update) | async-done | bytes 8388624 | tf_op jit(solution)/shard_map/all_gather | solution.py:45
  204.0 3.9 reduce_sum.29
  207.9 0.1 copy.11
  208.1 11.7 %cholesky.50 = f32[128,128]{1,0:T(8,128)S(1)} custom-call(f32[128,128]{1,0:T(8,128)S(1)} %cholesky.118), custom_call_target="Cholesky" | custom-call | tf_op jit(solution)/shard_map/jit(cholesky)/cholesky | solution.py:44
  219.9 9.8 %custom-call.16 = f32[1,128,128]{1,2,0:T(8,128)S(1)} custom-call(f32[1,128,128]{2,1,0:T(8,128)S(1)} %get-tuple-element.33), custom_call_target="InvertDiagBlocksLowerTriangular" | custom-call | tf_op jit(solution)/shard_map/jit(cholesky)/cholesky | solution.py:44
  229.7 0.2 constant_dynamic-update-slice_fusion
  229.9 0.3 convolution_subtract_fusion.2
  230.2 11.7 %cholesky.105 = f32[128,128]{1,0:T(8,128)S(1)} custom-call(f32[128,128]{1,0:T(8,128)S(1)} %convolution_subtract_fusion.2), custom_call_target="Cholesky" | custom-call | tf_op jit(solution)/shard_map/jit(cholesky)/cholesky | solution.py:44
  241.9 0.7 compare_reduce_fusion
  244.0 0.1 triangular_solve.72
  244.1 4.3 while.1
  244.3 0.6 fusion.44
  244.9 1.4 bitcast_dynamic-update-slice_fusion.2
  246.3 0.6 fusion.44
  246.9 1.4 bitcast_dynamic-update-slice_fusion.2
  248.4 19.7 %custom-call.17 = f32[2,128,128]{1,2,0:T(8,128)S(1)} custom-call(f32[2,128,128]{2,1,0:T(8,128)S(1)} %get-tuple-element.9), custom_call_target="InvertDiagBlocksLowerTriangular" | custom-call | tf_op jit(solution)/shard_map/triangular_solve | solution.py:24
  268.1 2.3 fusion.13
  270.4 3.0 convolution_subtract_fusion
  273.4 1.1 fusion.27
  274.5 18.2 %fusion.3 = f32[256,4096]{1,0:T(8,128)} fusion(bf16[2048,4096]{1,0:T(8,128)(2,1)} %param.5, f32[4096]{0:T(1024)S(1)} %get-tuple-element.35, f32[4096]{0:T(1024)S(1)} %get-tuple-element.34, f32[128,2048]{1,0:T(8,128)S(1)} %fusion.27, f32[128,2048]{1,0:T(8,128)S(1)} %fusion.13), kind=kOutput, calls=%fused_computation.8 | convolution fusion | flops 25803882496 | bytes 23101440 | tf_op jit(solution)/shard_map/dot_general | solution.py:49
  292.7 0.0 all-reduce.7.cloned.1.call-update
  292.7 1.7 fusion.19
  294.4 2.0 convolution_subtract_fusion.1
  296.5 0.6 fusion.28
  297.1 0.1 fusion.18
  297.2 1.0 copy.14
  298.2 161.4 %all-reduce.7.cloned.1.call-done = f32[256,4096]{1,0:T(8,128)} async-done(((f32[256,4096]{1,0:T(8,128)}), f32[256,4096]{1,0:T(8,128)}) %all-reduce.7.cloned.1.call-update) | async-done | bytes 4194320 | tf_op jit(solution)/shard_map/psum | solution.py:50
  459.7 3.9 multiply_convert_fusion
  (11 shorter events, 0.2 us)
Async XLA Ops:
  7.2 86.6 %copy-start = (bf16[4096,256]{1,0:T(8,128)(2,1)S(1)}, bf16[4096,256]{1,0:T(8,128)(2,1)}, u32[]{:S(2)}) copy-start(bf16[4096,256]{1,0:T(8,128)(2,1)} %param.6) | copy-start | bytes 6291460
  7.2 86.4 %copy-start.2 = (s32[4096]{0:T(1024)S(1)}, s32[4096]{0:T(1024)}, u32[]{:S(2)}) copy-start(s32[4096]{0:T(1024)} %param.8) | copy-start | bytes 49156
  7.2 86.4 %copy-start.3 = (f32[16]{0:T(128)S(1)}, f32[16]{0:T(128)}, u32[]{:S(2)}) copy-start(f32[16]{0:T(128)} %param.9) | copy-start | bytes 196
  7.2 86.6 %copy-start.1 = (s32[4096]{0:T(1024)S(1)}, s32[4096]{0:T(1024)}, u32[]{:S(2)}) copy-start(s32[4096]{0:T(1024)} %param.7) | copy-start | bytes 49156
  7.2 113.7 %all-reduce.5.cloned.1.call-start = ((), (), s32[]{:S(2)}) async-start(), calls=%async_computation | async-start | bytes 4194304 | tf_op jit(solution)/shard_map/psum | solution.py:42
  103.7 100.3 %all-gather.3.cloned.1.call-start = ((), (), s32[]{:S(2)}) async-start(), calls=%async_computation.2 | async-start | bytes 8650752 | tf_op jit(solution)/shard_map/all_gather | solution.py:45
  125.2 334.4 %all-reduce.7.cloned.1.call-start = ((), (), s32[]{:S(2)}) async-start(), calls=%async_computation.1 | async-start | bytes 8388608 | tf_op jit(solution)/shard_map/psum | solution.py:50
Sparse Core Ops, SparseCore 0:
  103.8 17.0 all-reduce.4
  125.4 78.5 all-gather.2
  292.9 166.7 all-reduce.6
